TPU v7x, 32 devices: a whole 2x2x4 slice. The times are simulated.
32 devices in a mesh: gx: 8 (over z, core), gy: 4 (over y, x).
Axes of the slice: x: 2, y: 2, z: 4, core: 2. Of those that a mesh axis runs over, the one named last changes fastest.
Arguments:
- pdf_old: float32 [4096, 19, 256], P(('gx', 'gy')), may hold values from -3 to 3
- tile_target: int32 [4096], P(('gx', 'gy')), may hold values from 0 to 4095, as said below
- porosity: float32 [128, 64, 128], P(('gx', 'gy')), may hold values from 0 to 0.6
- relaxation: float32 [128, 64, 128], P(('gx', 'gy')), may hold values from 0.6 to 1.8
- solid_mask: int32 [128, 64, 128], P('gx', 'gy'), may hold values 0 or 1
- force: float32 [3], replicated, may hold values from -0.1 to 0.1
Outputs:
- deviation_out: float32 [19, 128, 64, 128], P(None, 'gx', 'gy')
Inputs may be any that keep to these rules, and one draw needn't show every extreme that they name: tile_target holds every tile index once. The tiles of one device go to at most 8 of their number to any one device (device = tile index // 128), and in every draw some device sends exactly 8 tiles to some device.
All inputs are finite; a program needn't handle non-finite values. No bound on the sum of `solid_mask` on one device may be relied on, other than what follows from the above.
Results may differ from a plain program's by a relative error of at most 0.00023.
Values sent between devices are 32-bit elements; how exact they have to be, the bound alone decides.
A program may use at most 64 MiB of HBM per device.

v0:
```python
import functools

import jax
import jax.numpy as jnp
from jax import lax
from jax.experimental import pallas as pl
from jax.experimental.pallas import tpu as pltpu
from jax.sharding import PartitionSpec as P

STEPS = 2
VELOCITY = (
    (0, 0, 0),
    (1, 0, 0),
    (-1, 0, 0),
    (0, 1, 0),
    (0, -1, 0),
    (0, 0, 1),
    (0, 0, -1),
    (1, 1, 0),
    (-1, -1, 0),
    (1, -1, 0),
    (-1, 1, 0),
    (1, 0, 1),
    (-1, 0, -1),
    (1, 0, -1),
    (-1, 0, 1),
    (0, 1, 1),
    (0, -1, -1),
    (0, 1, -1),
    (0, -1, 1),
)
MAGIC = 0.1875
MESH = pl.DeviceIdType.MESH
LANES = 128
PAD = 8
MIB = 1 << 20


def moving(axis, sign):
    return [q for q in range(19) if VELOCITY[q][axis] == sign]


CORNERS = [(q, VELOCITY[q][0], VELOCITY[q][1]) for q in range(19) if VELOCITY[q][0] * VELOCITY[q][1] != 0]


def collide(dev, porosity, omega, mask, force):
    solid = porosity + mask.astype(jnp.float32) * (1.0 - porosity)
    fluid = 1.0 - solid
    omega_minus = (2.0 - omega) / (1.0 + (2.0 * MAGIC - 0.5) * omega)
    sums = {q: dev[q] + dev[q + 1] for q in range(1, 19, 2)}
    gaps = {q: dev[q] - dev[q + 1] for q in range(1, 19, 2)}
    axis_sum = sums[1] + sums[3] + sums[5]
    diagonal_sum = (sums[7] + sums[9]) + (sums[11] + sums[13]) + (sums[15] + sums[17])
    density = dev[0] * (1.0 / 3.0) + axis_sum * (1.0 / 18.0) + diagonal_sum * (1.0 / 36.0)
    flow = []
    for axis in range(3):
        straight = gaps[1 + 2 * axis]
        slanted = None
        for q in range(7, 19, 2):
            if VELOCITY[q][axis]:
                term = gaps[q] if VELOCITY[q][axis] > 0 else -gaps[q]
                slanted = term if slanted is None else slanted + term
        flow.append(straight * (1.0 / 18.0) + slanted * (1.0 / 36.0) + 0.5 * force[axis])
    base = density - 1.5 * (flow[0] * flow[0] + flow[1] * flow[1] + flow[2] * flow[2])
    pull = fluid * omega
    keep = 0.5 * (1.0 - pull)
    turn = 0.5 * (fluid * (1.0 - omega_minus) - solid)
    push = [3.0 * fluid * (omega_minus * flow[axis] + force[axis]) for axis in range(3)]

    def along(vector, velocity):
        total = None
        for axis in range(3):
            if velocity[axis]:
                term = vector[axis] if velocity[axis] > 0 else -vector[axis]
                total = term if total is None else total + term
        return total

    post = [None] * 19
    post[0] = dev[0] + pull * (base - dev[0])
    for q in range(1, 19, 2):
        speed = along(flow, VELOCITY[q])
        even = keep * sums[q] + pull * (base + 4.5 * (speed * speed))
        odd = turn * gaps[q] + along(push, VELOCITY[q])
        post[q] = even + odd
        post[q + 1] = even - odd
    return post


def route_kernel(held, capacity, target, table, labels, count):
    owners = labels.shape[0]
    labels[...] = jnp.full(labels.shape, -1, jnp.int32)

    def clear(d, carry):
        count[d] = 0
        for k in range(capacity):
            table[d * capacity + k] = 0
        return carry

    lax.fori_loop(0, owners, clear, 0)

    def place(k, carry):
        goal = target[k]
        owner = lax.div(goal, held)
        rank = count[owner]
        count[owner] = rank + 1
        table[owner * capacity + rank] = k
        labels[owner, pl.ds(rank, 1), :] = jnp.full((1, LANES), goal - owner * held, jnp.int32)
        return carry

    lax.fori_loop(0, held, place, 0)


def route(target, owners, capacity):
    return pl.pallas_call(
        functools.partial(route_kernel, target.shape[0], capacity),
        out_shape=(
            jax.ShapeDtypeStruct((owners * capacity,), jnp.int32),
            jax.ShapeDtypeStruct((owners, capacity, LANES), jnp.int32),
        ),
        in_specs=[pl.BlockSpec(memory_space=pltpu.SMEM)],
        out_specs=[pl.BlockSpec(memory_space=pltpu.SMEM), pl.BlockSpec(memory_space=pltpu.VMEM)],
        scratch_shapes=[pltpu.SMEM((owners,), jnp.int32)],
        name="route_tiles",
    )(target)


def flow_kernel(nx, ny, capacity, parts,
                table, force, labels, pdf, poro, relax, mask, out,
                halves, packed, arrived, places, slots, slot_of, plane, poro_block, relax_block,
                first, second, x_send, y_send, c_send, x_recv, y_recv, c_recv,
                tile_send, tile_recv, label_send, label_recv, cell_send, cell_recv, own, send, recv):
    n = nx * ny
    held = pdf.shape[1]
    depth = capacity * parts
    a, b = lax.axis_index("gx"), lax.axis_index("gy")
    me = a * ny + b
    bx, by = mask.shape[:2]
    slab = poro.shape[0]
    half = nx // 2
    loads = [
        pltpu.make_async_copy(pdf.at[:, :, pl.ds(r * LANES, LANES)], halves.at[r], own.at[r])
        for r in range(parts)
    ]
    mine = [
        pltpu.make_async_copy(
            whole.at[:, pl.ds(b * by, by), :], block.at[pl.ds(b * slab, slab)], own.at[parts + i]
        )
        for i, (whole, block) in enumerate(((poro, poro_block), (relax, relax_block)))
    ]
    for copy in loads + mine:
        copy.start()

    def partner(o, sign):
        side = 1 - lax.rem(o // (half * ny), 2)
        i = lax.rem(o // ny, half)
        j = lax.rem(o, ny)
        other = lax.rem(a // half + side, 2) * half + lax.rem(lax.rem(a, half) + half + sign * i, half)
        return other, lax.rem(b + ny + sign * j, ny)

    last = n // 2
    order = lambda step: step + lax.div(step, last)
    barrier = pltpu.get_barrier_semaphore()

    def greet(step, carry):
        pl.semaphore_signal(barrier, inc=1, device_id=partner(order(step), 1), device_id_type=MESH)
        return carry

    lax.fori_loop(0, n - 1, greet, 0)
    pl.semaphore_wait(barrier, n - 1)

    def tile_copies(o):
        to, source = partner(o, 1), partner(o, -1)
        goal = to[0] * ny + to[1]
        return (
            pltpu.make_async_remote_copy(
                src_ref=labels.at[goal], dst_ref=places.at[me],
                send_sem=label_send.at[o], recv_sem=label_recv.at[o],
                device_id=to, device_id_type=MESH,
            ),
            pltpu.make_async_remote_copy(
                src_ref=packed.at[goal], dst_ref=arrived.at[me],
                send_sem=tile_send.at[o], recv_sem=tile_recv.at[o],
                device_id=to, device_id_type=MESH,
            ),
        )

    def tile_arrivals(o):
        to, source = partner(o, 1), partner(o, -1)
        origin = source[0] * ny + source[1]
        return (
            pltpu.make_async_remote_copy(
                src_ref=labels.at[origin], dst_ref=places.at[origin],
                send_sem=label_send.at[o], recv_sem=label_recv.at[o],
                device_id=to, device_id_type=MESH,
            ),
            pltpu.make_async_remote_copy(
                src_ref=packed.at[origin], dst_ref=arrived.at[origin],
                send_sem=tile_send.at[o], recv_sem=tile_recv.at[o],
                device_id=to, device_id_type=MESH,
            ),
        )

    def cell_copies(o, source, target):
        return [
            pltpu.make_async_remote_copy(
                src_ref=whole.at[:, pl.ds(target * by, by), :],
                dst_ref=block.at[pl.ds(source * slab, slab)],
                send_sem=cell_send.at[2 * o + i], recv_sem=cell_recv.at[2 * o + i],
                device_id=(a, target), device_id_type=MESH,
            )
            for i, (whole, block) in enumerate(((poro, poro_block), (relax, relax_block)))
        ]

    for copy in loads:
        copy.wait()
    flat = [halves.at[r].reshape(19 * held, LANES) for r in range(parts)]

    def fill(block, goal):
        for k in range(capacity):
            tile = table[goal * capacity + k]
            for r in range(parts):
                block[goal if block is packed else me, pl.ds(k * parts + r, 19, stride=depth), :] = (
                    flat[r][pl.ds(tile, 19, stride=held), :]
                )

    def send_tiles(step, carry):
        o = order(step)
        to = partner(o, 1)
        fill(packed, to[0] * ny + to[1])
        for copy in tile_copies(o):
            copy.start()
        return carry

    lax.fori_loop(0, n - 1, send_tiles, 0)
    for o in range(1, ny):
        for copy in cell_copies(o, b, lax.rem(b + o, ny)):
            copy.start()
    fill(arrived, me)
    places[me] = labels[me]
    for copy in mine:
        copy.wait()
    for o in range(1, ny):
        for copy in cell_copies(o, lax.rem(b + ny - o, ny), lax.rem(b + o, ny)):
            copy.wait_send()
            copy.wait_recv()

    def take_tiles(step, carry):
        for copy in tile_arrivals(order(step)):
            copy.wait_recv()
        return carry

    lax.fori_loop(0, n - 1, take_tiles, 0)

    lane = lax.broadcasted_iota(jnp.int32, (1, LANES), 1)

    def invert(d, total):
        for k in range(capacity):
            total = jnp.maximum(
                total, jnp.where(places[d, k : k + 1, :] == lane, d * capacity + k, 0)
            )
        return total

    slots[...] = lax.fori_loop(0, n, invert, jnp.zeros((1, LANES), jnp.int32))
    down = pltpu.make_async_copy(slots, slot_of, own.at[parts + 2])
    down.start()
    down.wait()
    forces = [force[axis] for axis in range(3)]
    strips = by // parts

    def start(x, carry):
        for j in range(strips):
            slot = slot_of[0, x * strips + j]
            source = lax.div(slot, capacity)
            row = (slot - source * capacity) * parts
            for r in range(parts):
                plane[pl.ds(j * parts + r, 19, stride=by), :] = arrived[
                    source, pl.ds(row + r, 19, stride=depth), :
                ]
        for h in range(0, by, 8):
            dev = [plane[q * by + h : q * by + h + 8, :] for q in range(19)]
            done = collide(
                dev, poro_block[x, h : h + 8], relax_block[x, h : h + 8], mask[x, h : h + 8], forces
            )
            for q in range(19):
                first[q, x + 1, PAD + h : PAD + h + 8, :] = done[q]
        return carry

    lax.fori_loop(0, bx, start, 0)

    ring_x = {1: lax.rem(a + 1, nx), -1: lax.rem(a + nx - 1, nx), 0: a}
    ring_y = {1: lax.rem(b + 1, ny), -1: lax.rem(b + ny - 1, ny), 0: b}
    from_x, to_x = {1: bx, -1: 1}, {1: 0, -1: bx + 1}
    from_y, to_y = {1: PAD + by - 1, -1: PAD}, {1: PAD - 1, -1: PAD + by}

    def copies(turn):
        plan = [(x_send, x_recv, i, (sign, 0)) for i, sign in enumerate((1, -1))]
        plan += [(y_send, y_recv, i, (0, sign)) for i, sign in enumerate((1, -1))]
        plan += [(c_send, c_recv, i, (dx, dy)) for i, (q, dx, dy) in enumerate(CORNERS)]
        return [
            pltpu.make_async_remote_copy(
                src_ref=source.at[turn, i], dst_ref=goal.at[turn, i],
                send_sem=send.at[turn, k], recv_sem=recv.at[turn, k],
                device_id=(ring_x[dx], ring_y[dy]), device_id_type=MESH,
            )
            for k, (source, goal, i, (dx, dy)) in enumerate(plan)
        ]

    def swap(turn, field):
        for i, sign in enumerate((1, -1)):
            for j, q in enumerate(moving(0, sign)):
                x_send[turn, i, j] = field[q, from_x[sign], PAD : PAD + by, :]

        def gather(x, carry):
            for i, sign in enumerate((1, -1)):
                for j, q in enumerate(moving(1, sign)):
                    y_send[turn, i, j, pl.ds(x, 1), :] = field[
                        q, x + 1, from_y[sign] : from_y[sign] + 1, :
                    ]
            return carry

        lax.fori_loop(0, bx, gather, 0)
        for i, (q, dx, dy) in enumerate(CORNERS):
            c_send[turn, i, 0:1, :] = field[q, from_x[dx], from_y[dy] : from_y[dy] + 1, :]
        moves = copies(turn)
        for move in moves:
            move.start()
        for move in moves:
            move.wait()
        for i, sign in enumerate((1, -1)):
            for j, q in enumerate(moving(0, sign)):
                field[q, to_x[sign], PAD : PAD + by, :] = x_recv[turn, i, j]

        def spread(x, carry):
            for i, sign in enumerate((1, -1)):
                for j, q in enumerate(moving(1, sign)):
                    field[q, x + 1, to_y[sign] : to_y[sign] + 1, :] = y_recv[
                        turn, i, j, pl.ds(x, 1), :
                    ]
            return carry

        lax.fori_loop(0, bx, spread, 0)
        for i, (q, dx, dy) in enumerate(CORNERS):
            field[q, to_x[dx], to_y[dy] : to_y[dy] + 1, :] = c_recv[turn, i, 0:1, :]

    def streamed(field, q, x, h):
        dx, dy, dz = VELOCITY[q]
        window = field[q, x + 1 - dx, PAD + h - dy : PAD + h - dy + 8, :]
        return pltpu.roll(window, dz % LANES, 1) if dz else window

    swap(0, first)

    def middle(x, carry):
        for h in range(0, by, 8):
            dev = [streamed(first, q, x, h) for q in range(19)]
            done = collide(
                dev, poro_block[x, h : h + 8], relax_block[x, h : h + 8], mask[x, h : h + 8], forces
            )
            for q in range(19):
                second[q, x + 1, PAD + h : PAD + h + 8, :] = done[q]
        return carry

    lax.fori_loop(0, bx, middle, 0)
    swap(1, second)

    def finish(x, carry):
        for h in range(0, by, 8):
            for q in range(19):
                out[q, x, h : h + 8, :] = streamed(second, q, x, h)
        return carry

    lax.fori_loop(0, bx, finish, 0)

    def sent(step, carry):
        for copy in tile_copies(order(step)):
            copy.wait_send()
        return carry

    lax.fori_loop(0, n - 1, sent, 0)


def local(pdf_old, tile_target, porosity, relaxation, solid_mask, force):
    nx, ny = lax.axis_size("gx"), lax.axis_size("gy")
    n = nx * ny
    held, _, tile_cells = pdf_old.shape
    capacity = 2 * held // n
    bx, by, nz = solid_mask.shape
    parts = tile_cells // nz
    table, labels = route(tile_target, n, capacity)
    tiles = pltpu.VMEM((n, 19 * capacity * parts, nz), jnp.float32)
    block = pltpu.VMEM((bx, by, nz), jnp.float32)
    field = pltpu.VMEM((19, bx + 2, by + 2 * PAD, nz), jnp.float32)
    faces = [
        pltpu.VMEM((2, 2, 5, by, nz), jnp.float32),
        pltpu.VMEM((2, 2, 5, bx, nz), jnp.float32),
        pltpu.VMEM((2, 4, 8, nz), jnp.float32),
    ]
    return pl.pallas_call(
        functools.partial(flow_kernel, nx, ny, capacity, parts),
        out_shape=jax.ShapeDtypeStruct((19, bx, by, nz), jnp.float32),
        in_specs=[pl.BlockSpec(memory_space=pltpu.SMEM)] * 2
        + [pl.BlockSpec(memory_space=pltpu.VMEM)]
        + [pl.BlockSpec(memory_space=pl.ANY)] * 3
        + [pl.BlockSpec(memory_space=pltpu.VMEM)],
        out_specs=pl.BlockSpec(memory_space=pltpu.VMEM),
        scratch_shapes=[
            pltpu.VMEM((parts, 19, held, nz), jnp.float32),
            tiles,
            tiles,
            pltpu.VMEM(labels.shape, jnp.int32),
            pltpu.VMEM((1, LANES), jnp.int32),
            pltpu.SMEM((1, LANES), jnp.int32),
            pltpu.VMEM((19 * by, nz), jnp.float32),
            block,
            block,
            field,
            field,
        ]
        + faces
        + faces
        + [pltpu.SemaphoreType.DMA((n,))] * 4
        + [pltpu.SemaphoreType.DMA((2 * ny,))] * 2
        + [pltpu.SemaphoreType.DMA((parts + 3,))]
        + [pltpu.SemaphoreType.DMA((2, 8))] * 2,
        compiler_params=pltpu.CompilerParams(
            collective_id=0, has_side_effects=True, vmem_limit_bytes=48 * MIB
        ),
        name="exchange_and_flow",
    )(table, force, labels, jnp.transpose(pdf_old, (1, 0, 2)), porosity, relaxation, solid_mask)


def solution(mesh):
    return jax.shard_map(
        local,
        mesh=mesh,
        in_specs=(
            P(("gx", "gy"), None, None),
            P(("gx", "gy")),
            P(("gx", "gy"), None, None),
            P(("gx", "gy"), None, None),
            P("gx", "gy", None),
            P(),
        ),
        out_specs=P(None, "gx", "gy", None),
        check_vma=False,
    )
```

profile of v0, /device:TPU:0, one launch (start us, length us, event | category | flops | bytes accessed | tf_op | source)
XLA Modules:
  0.0 150.7 jit_solution(8447170673699941673)
XLA Ops:
  0.0 3.8 %route_tiles.1 = (s32[256]{0:T(256)}, s32[32,8,128]{2,1,0:T(8,128)}) custom-call(s32[128]{0:T(128)} %target.1), custom_call_target="tpu_custom_call" | custom-call | tf_op jit(solution)/shard_map/route_tiles/pallas_call | solution.py:114
  3.8 0.0 copy-start
  3.8 1.7 %copy-done = f32[128,19,256]{2,0,1:T(8,128)S(1)} copy-done((f32[128,19,256]{2,0,1:T(8,128)S(1)}, f32[128,19,256]{2,0,1:T(8,128)}, u32[]{:S(2)}) %copy-start) | copy-done | bytes 2490392
  5.5 0.0 copy-start.1
  5.5 0.9 copy-done.1
  6.4 0.0 copy-start.2
  6.4 0.9 copy-done.2
  7.3 0.0 copy-start.3
  7.3 0.9 copy-done.3
  8.2 0.0 copy-start.4
  8.2 0.9 copy-done.4
  9.1 0.0 copy-start.5
  9.1 0.7 copy-done.5
  9.7 0.0 copy-start.6
  9.7 0.7 copy-done.6
  10.4 138.8 %exchange_and_flow.1 = f32[19,16,16,128]{3,2,1,0:T(8,128)S(1)} custom-call(s32[256]{0:T(256)S(1)} %copy-done.5, f32[3]{0:T(128)S(1)} %copy-done.6, s32[32,8,128]{2,1,0:T(8,128)S(1)} %copy-done.4, f32[19,128,256]{2,1,0:T(8,128)S(1)} %bitcast.1, f32[4,64,128]{2,1,0:T(8,128)S(1)} %copy-done.1, f32[4,64,128]{2,1,0:T(8,128)S(1)} %copy-done.2, ...), custom_call_target="tpu_custom_call" | custom-call | tf_op jit(solution)/shard_map/exchange_and_flow/pallas_call | solution.py:397
  149.3 1.5 copy.8
Async XLA Ops:
  3.8 1.7 %copy-start = (f32[128,19,256]{2,0,1:T(8,128)S(1)}, f32[128,19,256]{2,0,1:T(8,128)}, u32[]{:S(2)}) copy-start(f32[128,19,256]{2,0,1:T(8,128)} %param.6) | copy-start | bytes 7471108
  5.5 0.9 copy-start.1
  6.4 0.9 copy-start.2
  7.3 0.9 copy-start.3
  8.2 0.9 copy-start.4
  9.1 0.7 copy-start.5
  9.7 0.7 copy-start.6
where the time goes:
time: 151 us
  Pallas kernels  143 us (95%)
  local copies, waits for them, and re-layouts  8.08 us (5%)
    pallas_call x1, Pallas kernels, local(): pl.pallas_call(functools.partial(flow_kernel, nx, ny, capacity, parts), o...  139 us
    unnamed x15, local copies, waits for them, and re-layouts  8.08 us
    pallas_call x1, Pallas kernels, route(): pl.pallas_call(functools.partial(route_kernel, target.shape[0], capacity)...  3.75 us

commit v1 on v0

--- a/solution.py
+++ b/solution.py
@@ -157,8 +157,10 @@
         other = lax.rem(a // half + side, 2) * half + lax.rem(lax.rem(a, half) + half + sign * i, half)
         return other, lax.rem(b + ny + sign * j, ny)
 
-    last = n // 2
-    order = lambda step: step + lax.div(step, last)
+    def order(step):
+        pair = step // 2
+        return pair + lax.rem(step, 2) * (n // 2 + 1)
+
     barrier = pltpu.get_barrier_semaphore()
 
     def greet(step, carry):
@@ -422,7 +424,7 @@
         + [pltpu.SemaphoreType.DMA((parts + 3,))]
         + [pltpu.SemaphoreType.DMA((2, 8))] * 2,
         compiler_params=pltpu.CompilerParams(
-            collective_id=0, has_side_effects=True, vmem_limit_bytes=48 * MIB
+            collective_id=0, has_side_effects=True, vmem_limit_bytes=62 * MIB
         ),
         name="exchange_and_flow",
     )(table, force, labels, jnp.transpose(pdf_old, (1, 0, 2)), porosity, relaxation, solid_mask)

time: 151 us -> 148 us (0.980)
  local copies, waits for them, and re-layouts: 8.08 us -> 3.37 us
    unnamed x15 -> x1, local copies, waits for them, and re-layouts: 8.08 us -> 3.37 us
    pallas_call x1, Pallas kernels: 139 us -> 141 us  [local(): pl.pallas_call(functools.partial(flow_kernel, nx, ny, capacity, parts), o...]
where the time goes in v1:
time: 148 us
  Pallas kernels  144 us (97%)
  local copies, waits for them, and re-layouts  3.37 us (2%)
    pallas_call x1, Pallas kernels, local(): pl.pallas_call(functools.partial(flow_kernel, nx, ny, capacity, parts), o...  141 us
    pallas_call x1, Pallas kernels, route(): pl.pallas_call(functools.partial(route_kernel, target.shape[0], capacity)...  3.75 us
    unnamed x1, local copies, waits for them, and re-layouts  3.37 us

profile of v1, /device:TPU:0, one launch (start us, length us, event | category | flops | bytes accessed | tf_op | source)
XLA Modules:
  0.0 147.8 jit_solution(13887678394807974837)
XLA Ops:
  0.0 3.8 %route_tiles.1 = (s32[256]{0:T(256)}, s32[32,8,128]{2,1,0:T(8,128)}) custom-call(s32[128]{0:T(128)} %target.1), custom_call_target="tpu_custom_call" | custom-call | tf_op jit(solution)/shard_map/route_tiles/pallas_call | solution.py:114
  3.8 140.6 %exchange_and_flow.1 = f32[19,16,16,128]{3,2,1,0:T(8,128)} custom-call(s32[256]{0:T(256)} %get-tuple-element.7.table, f32[3]{0:T(128)} %force.1, s32[32,8,128]{2,1,0:T(8,128)} %get-tuple-element.8.labels, f32[19,128,256]{2,1,0:T(8,128)} %bitcast.1, f32[4,64,128]{2,1,0:T(8,128)} %poro.1, f32[4,64,128]{2,1,0:T(8,128)} %relax.1, s32[16,16,128]{2,1,0:T(8,128)} %mask.1), custom_call_target="tpu_custom_call" | custom-call | tf_op jit(solution)/shard_map/exchange_and_flow/pallas_call | solution.py:399
  144.4 3.4 %copy.8 = f32[19,16,16,128]{3,2,1,0:T(8,128)} copy(f32[19,16,16,128]{3,2,1,0:T(8,128)} %exchange_and_flow.1) | data formatting | bytes 4980736

commit v2 on v1

--- a/solution.py
+++ b/solution.py
@@ -86,47 +86,31 @@
     return post
 
 
-def route_kernel(held, capacity, target, table, labels, count):
-    owners = labels.shape[0]
-    labels[...] = jnp.full(labels.shape, -1, jnp.int32)
-
-    def clear(d, carry):
-        count[d] = 0
-        for k in range(capacity):
-            table[d * capacity + k] = 0
-        return carry
-
-    lax.fori_loop(0, owners, clear, 0)
-
-    def place(k, carry):
-        goal = target[k]
-        owner = lax.div(goal, held)
-        rank = count[owner]
-        count[owner] = rank + 1
-        table[owner * capacity + rank] = k
-        labels[owner, pl.ds(rank, 1), :] = jnp.full((1, LANES), goal - owner * held, jnp.int32)
-        return carry
-
-    lax.fori_loop(0, held, place, 0)
-
-
-def route(target, owners, capacity):
-    return pl.pallas_call(
-        functools.partial(route_kernel, target.shape[0], capacity),
-        out_shape=(
-            jax.ShapeDtypeStruct((owners * capacity,), jnp.int32),
-            jax.ShapeDtypeStruct((owners, capacity, LANES), jnp.int32),
-        ),
-        in_specs=[pl.BlockSpec(memory_space=pltpu.SMEM)],
-        out_specs=[pl.BlockSpec(memory_space=pltpu.SMEM), pl.BlockSpec(memory_space=pltpu.VMEM)],
-        scratch_shapes=[pltpu.SMEM((owners,), jnp.int32)],
-        name="route_tiles",
-    )(target)
+def column(rows, diagonal):
+    return jnp.sum(jnp.where(diagonal, rows, 0), axis=1, keepdims=True)
+
+
+def fill_tables(held, capacity, goal, table, labels):
+    sub = lax.broadcasted_iota(jnp.int32, (held, LANES), 0)
+    lane = lax.broadcasted_iota(jnp.int32, (held, LANES), 1)
+    diagonal = sub == lane
+    goals = jnp.broadcast_to(goal[...], (held, LANES))
+    owners = lax.shift_right_logical(goals, held.bit_length() - 1)
+    inner = goals - owners * held
+    same = (column(owners, diagonal) == owners) & (sub < lane)
+    rank = jnp.sum(jnp.where(same, 1, 0), axis=0, keepdims=True)
+    slot = column(owners * capacity + rank, diagonal)
+    place = column(inner, diagonal)
+    for c in range(table.shape[0]):
+        hit = slot == lane + c * LANES
+        table[c : c + 1, :] = jnp.max(jnp.where(hit, sub, 0), axis=0, keepdims=True)
+        labels[c : c + 1, :] = jnp.max(jnp.where(hit, place, -1), axis=0, keepdims=True)
 
 
 def flow_kernel(nx, ny, capacity, parts,
-                table, force, labels, pdf, poro, relax, mask, out,
-                halves, packed, arrived, places, slots, slot_of, plane, poro_block, relax_block,
+                force, goal, pdf, poro, relax, mask_hbm, out,
+                table_rows, table, labels, gathered, mask, halves, packed, arrived, places, slots,
+                slot_of, plane, poro_block, relax_block,
                 first, second, x_send, y_send, c_send, x_recv, y_recv, c_recv,
                 tile_send, tile_recv, label_send, label_recv, cell_send, cell_recv, own, send, recv):
     n = nx * ny
@@ -147,6 +131,8 @@
         )
         for i, (whole, block) in enumerate(((poro, poro_block), (relax, relax_block)))
     ]
+    mine.append(pltpu.make_async_copy(mask_hbm, mask, own.at[parts + 2]))
+    down = pltpu.make_async_copy(table_rows, table, own.at[parts + 3])
     for copy in loads + mine:
         copy.start()
 
@@ -168,6 +154,9 @@
         return carry
 
     lax.fori_loop(0, n - 1, greet, 0)
+    fill_tables(held, capacity, goal, table_rows, labels)
+    down.start()
+    down.wait()
     pl.semaphore_wait(barrier, n - 1)
 
     def tile_copies(o):
@@ -175,7 +164,7 @@
         goal = to[0] * ny + to[1]
         return (
             pltpu.make_async_remote_copy(
-                src_ref=labels.at[goal], dst_ref=places.at[me],
+                src_ref=labels, dst_ref=places.at[me],
                 send_sem=label_send.at[o], recv_sem=label_recv.at[o],
                 device_id=to, device_id_type=MESH,
             ),
@@ -191,7 +180,7 @@
         origin = source[0] * ny + source[1]
         return (
             pltpu.make_async_remote_copy(
-                src_ref=labels.at[origin], dst_ref=places.at[origin],
+                src_ref=labels, dst_ref=places.at[origin],
                 send_sem=label_send.at[o], recv_sem=label_recv.at[o],
                 device_id=to, device_id_type=MESH,
             ),
@@ -219,7 +208,8 @@
 
     def fill(block, goal):
         for k in range(capacity):
-            tile = table[goal * capacity + k]
+            spot = goal * capacity + k
+            tile = table[spot // LANES, lax.rem(spot, LANES)]
             for r in range(parts):
                 block[goal if block is packed else me, pl.ds(k * parts + r, 19, stride=depth), :] = (
                     flat[r][pl.ds(tile, 19, stride=held), :]
@@ -238,7 +228,7 @@
         for copy in cell_copies(o, b, lax.rem(b + o, ny)):
             copy.start()
     fill(arrived, me)
-    places[me] = labels[me]
+    places[me] = labels[...]
     for copy in mine:
         copy.wait()
     for o in range(1, ny):
@@ -253,19 +243,24 @@
 
     lax.fori_loop(0, n - 1, take_tiles, 0)
 
-    lane = lax.broadcasted_iota(jnp.int32, (1, LANES), 1)
-
-    def invert(d, total):
-        for k in range(capacity):
-            total = jnp.maximum(
-                total, jnp.where(places[d, k : k + 1, :] == lane, d * capacity + k, 0)
-            )
-        return total
-
-    slots[...] = lax.fori_loop(0, n, invert, jnp.zeros((1, LANES), jnp.int32))
-    down = pltpu.make_async_copy(slots, slot_of, own.at[parts + 2])
-    down.start()
-    down.wait()
+    chunk, offset = (me * capacity) // LANES, lax.rem(me * capacity, LANES)
+
+    def collect(d, carry):
+        gathered[pl.ds(d, 1), :] = places[d, pl.ds(chunk, 1), :]
+        return carry
+
+    lax.fori_loop(0, n, collect, 0)
+    rows = gathered[...]
+    sender = lax.broadcasted_iota(jnp.int32, (n, LANES), 0)
+    lane = lax.broadcasted_iota(jnp.int32, (n, LANES), 1)
+    found = jnp.zeros((n, LANES), jnp.int32)
+    for k in range(capacity):
+        label = jnp.sum(jnp.where(lane == offset + k, rows, 0), axis=1, keepdims=True)
+        found = jnp.maximum(found, jnp.where(label == lane, sender * capacity + k, 0))
+    slots[...] = jnp.max(found, axis=0, keepdims=True)
+    lift = pltpu.make_async_copy(slots, slot_of, own.at[parts + 4])
+    lift.start()
+    lift.wait()
     forces = [force[axis] for axis in range(3)]
     strips = by // parts
 
@@ -387,7 +382,7 @@
     capacity = 2 * held // n
     bx, by, nz = solid_mask.shape
     parts = tile_cells // nz
-    table, labels = route(tile_target, n, capacity)
+    chunks = n * capacity // LANES
     tiles = pltpu.VMEM((n, 19 * capacity * parts, nz), jnp.float32)
     block = pltpu.VMEM((bx, by, nz), jnp.float32)
     field = pltpu.VMEM((19, bx + 2, by + 2 * PAD, nz), jnp.float32)
@@ -399,16 +394,19 @@
     return pl.pallas_call(
         functools.partial(flow_kernel, nx, ny, capacity, parts),
         out_shape=jax.ShapeDtypeStruct((19, bx, by, nz), jnp.float32),
-        in_specs=[pl.BlockSpec(memory_space=pltpu.SMEM)] * 2
-        + [pl.BlockSpec(memory_space=pltpu.VMEM)]
-        + [pl.BlockSpec(memory_space=pl.ANY)] * 3
-        + [pl.BlockSpec(memory_space=pltpu.VMEM)],
+        in_specs=[pl.BlockSpec(memory_space=pltpu.SMEM), pl.BlockSpec(memory_space=pltpu.VMEM)]
+        + [pl.BlockSpec(memory_space=pl.ANY)] * 4,
         out_specs=pl.BlockSpec(memory_space=pltpu.VMEM),
         scratch_shapes=[
+            pltpu.VMEM((chunks, LANES), jnp.int32),
+            pltpu.SMEM((chunks, LANES), jnp.int32),
+            pltpu.VMEM((chunks, LANES), jnp.int32),
+            pltpu.VMEM((n, LANES), jnp.int32),
+            pltpu.VMEM((bx, by, nz), jnp.int32),
             pltpu.VMEM((parts, 19, held, nz), jnp.float32),
             tiles,
             tiles,
-            pltpu.VMEM(labels.shape, jnp.int32),
+            pltpu.VMEM((n, chunks, LANES), jnp.int32),
             pltpu.VMEM((1, LANES), jnp.int32),
             pltpu.SMEM((1, LANES), jnp.int32),
             pltpu.VMEM((19 * by, nz), jnp.float32),
@@ -421,13 +419,20 @@
         + faces
         + [pltpu.SemaphoreType.DMA((n,))] * 4
         + [pltpu.SemaphoreType.DMA((2 * ny,))] * 2
-        + [pltpu.SemaphoreType.DMA((parts + 3,))]
+        + [pltpu.SemaphoreType.DMA((parts + 5,))]
         + [pltpu.SemaphoreType.DMA((2, 8))] * 2,
         compiler_params=pltpu.CompilerParams(
             collective_id=0, has_side_effects=True, vmem_limit_bytes=62 * MIB
         ),
         name="exchange_and_flow",
-    )(table, force, labels, jnp.transpose(pdf_old, (1, 0, 2)), porosity, relaxation, solid_mask)
+    )(
+        force,
+        tile_target.reshape(1, held),
+        jnp.transpose(pdf_old, (1, 0, 2)),
+        porosity,
+        relaxation,
+        solid_mask,
+    )
 
 
 def solution(mesh):

time: 148 us -> 142 us (0.959)
  Pallas kernels: 144 us -> 138 us
    pallas_call x1 -> x0, Pallas kernels: 3.75 us -> none  [route(): pl.pallas_call(functools.partial(route_kernel, target.shape[0], capacity)...]
    pallas_call x1, Pallas kernels: 141 us -> 138 us  [local(): pl.pallas_call(functools.partial(flow_kernel, nx, ny, capacity, parts), o...]
where the time goes in v2:
time: 142 us
  Pallas kernels  138 us (97%)
  local copies, waits for them, and re-layouts  3.37 us (2%)
    pallas_call x1, Pallas kernels, local(): pl.pallas_call(functools.partial(flow_kernel, nx, ny, capacity, parts), o...  138 us
    unnamed x1, local copies, waits for them, and re-layouts  3.37 us

profile of v2, /device:TPU:0, one launch (start us, length us, event | category | flops | bytes accessed | tf_op | source)
XLA Modules:
  0.0 141.6 jit_solution(14437578718028556037)
XLA Ops:
  0.0 138.2 %exchange_and_flow.1 = f32[19,16,16,128]{3,2,1,0:T(8,128)} custom-call(f32[3]{0:T(128)} %force.1, s32[1,128]{1,0:T(1,128)} %bitcast.3, f32[19,128,256]{2,1,0:T(8,128)} %bitcast.2, f32[4,64,128]{2,1,0:T(8,128)} %poro.1, f32[4,64,128]{2,1,0:T(8,128)} %relax.1, s32[16,16,128]{2,1,0:T(8,128)} %mask_hbm.1), custom_call_target="tpu_custom_call" | custom-call | tf_op jit(solution)/shard_map/exchange_and_flow/pallas_call | solution.py:394
  138.2 3.4 %copy.8 = f32[19,16,16,128]{3,2,1,0:T(8,128)} copy(f32[19,16,16,128]{3,2,1,0:T(8,128)} %exchange_and_flow.1) | data formatting | bytes 4980736

commit v3 on v2

--- a/solution.py
+++ b/solution.py
@@ -107,8 +107,79 @@
         labels[c : c + 1, :] = jnp.max(jnp.where(hit, place, -1), axis=0, keepdims=True)
 
 
+def reach(bx, by):
+    return {1: 0, -1: bx + 1}, {1: PAD - 1, -1: PAD + by}
+
+
+def unpack_faces(field, x_face, y_face, c_face, bx, by):
+    to_x, to_y = reach(bx, by)
+    for i, sign in enumerate((1, -1)):
+        for j, q in enumerate(moving(0, sign)):
+            field[q, to_x[sign], PAD : PAD + by, :] = x_face[i, j]
+
+    def spread(x, carry):
+        for i, sign in enumerate((1, -1)):
+            for j, q in enumerate(moving(1, sign)):
+                field[q, x + 1, to_y[sign] : to_y[sign] + 1, :] = y_face[i, j, pl.ds(x, 1), :]
+        return carry
+
+    lax.fori_loop(0, bx, spread, 0)
+    for i, (q, dx, dy) in enumerate(CORNERS):
+        field[q, to_x[dx], to_y[dy] : to_y[dy] + 1, :] = c_face[i, 0:1, :]
+
+
+def streamed(field, q, x, h):
+    dx, dy, dz = VELOCITY[q]
+    window = field[q, x + 1 - dx, PAD + h - dy : PAD + h - dy + 8, :]
+    return pltpu.roll(window, dz % LANES, 1) if dz else window
+
+
+def finish_kernel(pieces, middle, x_face, y_face, c_face, out, field, stage, x_in, y_in, c_in,
+                  load_sem, store_sem, face_sem):
+    bx, by = out.shape[1:3]
+    size = bx // pieces
+    loads = [
+        pltpu.make_async_copy(
+            middle.at[:, pl.ds(c * size, size)],
+            field.at[:, pl.ds(1 + c * size, size), pl.ds(PAD, by), :],
+            load_sem.at[c],
+        )
+        for c in range(pieces)
+    ]
+    stores = [
+        pltpu.make_async_copy(
+            stage.at[:, pl.ds(c * size, size)], out.at[:, pl.ds(c * size, size)], store_sem.at[c]
+        )
+        for c in range(pieces)
+    ]
+    faces = [
+        pltpu.make_async_copy(face, ref, face_sem.at[i])
+        for i, (face, ref) in enumerate(((x_face, x_in), (y_face, y_in), (c_face, c_in)))
+    ]
+    for copy in faces + loads:
+        copy.start()
+    for copy in faces:
+        copy.wait()
+    unpack_faces(field, x_in, y_in, c_in, bx, by)
+    loads[0].wait()
+
+    def plane(x, carry):
+        for h in range(0, by, 8):
+            for q in range(19):
+                stage[q, x, h : h + 8, :] = streamed(field, q, x, h)
+        return carry
+
+    for c in range(pieces):
+        if c + 1 < pieces:
+            loads[c + 1].wait()
+        lax.fori_loop(c * size, (c + 1) * size, plane, 0)
+        stores[c].start()
+    for store in stores:
+        store.wait()
+
+
 def flow_kernel(nx, ny, capacity, parts,
-                force, goal, pdf, poro, relax, mask_hbm, out,
+                force, goal, pdf, poro, relax, mask_hbm, middle, x_out, y_out, c_out,
                 table_rows, table, labels, gathered, mask, halves, packed, arrived, places, slots,
                 slot_of, plane, poro_block, relax_block,
                 first, second, x_send, y_send, c_send, x_recv, y_recv, c_recv,
@@ -286,8 +357,7 @@
 
     ring_x = {1: lax.rem(a + 1, nx), -1: lax.rem(a + nx - 1, nx), 0: a}
     ring_y = {1: lax.rem(b + 1, ny), -1: lax.rem(b + ny - 1, ny), 0: b}
-    from_x, to_x = {1: bx, -1: 1}, {1: 0, -1: bx + 1}
-    from_y, to_y = {1: PAD + by - 1, -1: PAD}, {1: PAD - 1, -1: PAD + by}
+    from_x, from_y = {1: bx, -1: 1}, {1: PAD + by - 1, -1: PAD}
 
     def copies(turn):
         plan = [(x_send, x_recv, i, (sign, 0)) for i, sign in enumerate((1, -1))]
@@ -302,7 +372,7 @@
             for k, (source, goal, i, (dx, dy)) in enumerate(plan)
         ]
 
-    def swap(turn, field):
+    def send_faces(turn, field):
         for i, sign in enumerate((1, -1)):
             for j, q in enumerate(moving(0, sign)):
                 x_send[turn, i, j] = field[q, from_x[sign], PAD : PAD + by, :]
@@ -318,54 +388,69 @@
         lax.fori_loop(0, bx, gather, 0)
         for i, (q, dx, dy) in enumerate(CORNERS):
             c_send[turn, i, 0:1, :] = field[q, from_x[dx], from_y[dy] : from_y[dy] + 1, :]
-        moves = copies(turn)
-        for move in moves:
+        for move in copies(turn):
             move.start()
-        for move in moves:
+
+    def take_faces(turn, field):
+        for move in copies(turn):
             move.wait()
-        for i, sign in enumerate((1, -1)):
-            for j, q in enumerate(moving(0, sign)):
-                field[q, to_x[sign], PAD : PAD + by, :] = x_recv[turn, i, j]
-
-        def spread(x, carry):
-            for i, sign in enumerate((1, -1)):
-                for j, q in enumerate(moving(1, sign)):
-                    field[q, x + 1, to_y[sign] : to_y[sign] + 1, :] = y_recv[
-                        turn, i, j, pl.ds(x, 1), :
-                    ]
-            return carry
-
-        lax.fori_loop(0, bx, spread, 0)
-        for i, (q, dx, dy) in enumerate(CORNERS):
-            field[q, to_x[dx], to_y[dy] : to_y[dy] + 1, :] = c_recv[turn, i, 0:1, :]
-
-    def streamed(field, q, x, h):
-        dx, dy, dz = VELOCITY[q]
-        window = field[q, x + 1 - dx, PAD + h - dy : PAD + h - dy + 8, :]
-        return pltpu.roll(window, dz % LANES, 1) if dz else window
-
-    swap(0, first)
-
-    def middle(x, carry):
+        unpack_faces(field, x_recv.at[turn], y_recv.at[turn], c_recv.at[turn], bx, by)
+
+    def block(x, h):
+        dev = [streamed(first, q, x, h) for q in range(19)]
+        done = collide(
+            dev, poro_block[x, h : h + 8], relax_block[x, h : h + 8], mask[x, h : h + 8], forces
+        )
+        for q in range(19):
+            second[q, x + 1, PAD + h : PAD + h + 8, :] = done[q]
+
+    def second_step(x, carry):
         for h in range(0, by, 8):
-            dev = [streamed(first, q, x, h) for q in range(19)]
-            done = collide(
-                dev, poro_block[x, h : h + 8], relax_block[x, h : h + 8], mask[x, h : h + 8], forces
-            )
-            for q in range(19):
-                second[q, x + 1, PAD + h : PAD + h + 8, :] = done[q]
-        return carry
-
-    lax.fori_loop(0, bx, middle, 0)
-    swap(1, second)
-
-    def finish(x, carry):
-        for h in range(0, by, 8):
-            for q in range(19):
-                out[q, x, h : h + 8, :] = streamed(second, q, x, h)
-        return carry
-
-    lax.fori_loop(0, bx, finish, 0)
+            block(x, h)
+        return carry
+
+    tall = by + 2 * PAD
+    first_rows = first.reshape(19 * (bx + 2) * tall, LANES)
+    second_rows = second.reshape(19 * (bx + 2) * tall, LANES)
+    cell_rows = [ref.reshape(bx * by, LANES) for ref in (poro_block, relax_block, mask)]
+
+    def edge(row, x):
+        dev = []
+        for q in range(19):
+            dx, dy, dz = VELOCITY[q]
+            begin = (q * (bx + 2) + x + 1 - dx) * tall + PAD + row - dy
+            window = first_rows[pl.ds(begin, 8, stride=tall), :]
+            dev.append(pltpu.roll(window, dz % LANES, 1) if dz else window)
+        cells = [ref[pl.ds(x * by + row, 8, stride=by), :] for ref in cell_rows]
+        done = collide(dev, *cells, forces)
+        for q in range(19):
+            begin = (q * (bx + 2) + x + 1) * tall + PAD + row
+            second_rows[pl.ds(begin, 8, stride=tall), :] = done[q]
+
+    send_faces(0, first)
+    lax.fori_loop(1, bx - 1, second_step, 0)
+    take_faces(0, first)
+    for x in (0, bx - 1):
+        second_step(x, 0)
+    for x in range(0, bx, 8):
+        for row in (0, by - 1):
+            edge(row, x)
+    keep = pltpu.make_async_copy(
+        second.at[:, pl.ds(1, bx), pl.ds(PAD, by), :], middle, own.at[0]
+    )
+    keep.start()
+    send_faces(1, second)
+    for move in copies(1):
+        move.wait()
+    faces = [
+        pltpu.make_async_copy(ref.at[1], face, own.at[1 + i])
+        for i, (ref, face) in enumerate(((x_recv, x_out), (y_recv, y_out), (c_recv, c_out)))
+    ]
+    for copy in faces:
+        copy.start()
+    for copy in faces:
+        copy.wait()
+    keep.wait()
 
     def sent(step, carry):
         for copy in tile_copies(order(step)):
@@ -391,12 +476,15 @@
         pltpu.VMEM((2, 2, 5, bx, nz), jnp.float32),
         pltpu.VMEM((2, 4, 8, nz), jnp.float32),
     ]
-    return pl.pallas_call(
+    result = jax.ShapeDtypeStruct((19, bx, by, nz), jnp.float32)
+    slim = [(2, 5, by, nz), (2, 5, bx, nz), (4, 8, nz)]
+    halos = [jax.ShapeDtypeStruct(shape, jnp.float32) for shape in slim]
+    middle = pl.pallas_call(
         functools.partial(flow_kernel, nx, ny, capacity, parts),
-        out_shape=jax.ShapeDtypeStruct((19, bx, by, nz), jnp.float32),
+        out_shape=[result] + halos,
         in_specs=[pl.BlockSpec(memory_space=pltpu.SMEM), pl.BlockSpec(memory_space=pltpu.VMEM)]
         + [pl.BlockSpec(memory_space=pl.ANY)] * 4,
-        out_specs=pl.BlockSpec(memory_space=pltpu.VMEM),
+        out_specs=[pl.BlockSpec(memory_space=pl.ANY)] * 4,
         scratch_shapes=[
             pltpu.VMEM((chunks, LANES), jnp.int32),
             pltpu.SMEM((chunks, LANES), jnp.int32),
@@ -433,6 +521,19 @@
         relaxation,
         solid_mask,
     )
+    pieces = 4
+    return pl.pallas_call(
+        functools.partial(finish_kernel, pieces),
+        out_shape=result,
+        in_specs=[pl.BlockSpec(memory_space=pl.ANY)] * 4,
+        out_specs=pl.BlockSpec(memory_space=pl.ANY),
+        scratch_shapes=[field, pltpu.VMEM((19, bx, by, nz), jnp.float32)]
+        + [pltpu.VMEM(shape, jnp.float32) for shape in slim]
+        + [pltpu.SemaphoreType.DMA((pieces,))] * 2
+        + [pltpu.SemaphoreType.DMA((3,))],
+        compiler_params=pltpu.CompilerParams(vmem_limit_bytes=62 * MIB),
+        name="last_stream",
+    )(*middle)
 
 
 def solution(mesh):

time: 142 us -> 138 us (0.972)
  local copies, waits for them, and re-layouts: 3.37 us -> 0 us
    pallas_call x1, Pallas kernels: 138 us -> 134 us  [local(): pl.pallas_call(functools.partial(flow_kernel, nx, ny, capacity, parts), o...]
    pallas_call x0 -> x1, Pallas kernels: none -> 3.79 us  [local(): pl.pallas_call(functools.partial(finish_kernel, pieces), out_shape=result...]
    unnamed x1 -> x0, local copies, waits for them, and re-layouts: 3.37 us -> none
where the time goes in v3:
time: 138 us
  Pallas kernels  138 us (100%)
    pallas_call x1, Pallas kernels, local(): pl.pallas_call(functools.partial(flow_kernel, nx, ny, capacity, parts), o...  134 us
    pallas_call x1, Pallas kernels, local(): pl.pallas_call(functools.partial(finish_kernel, pieces), out_shape=result...  3.79 us

profile of v3, /device:TPU:0, one launch (start us, length us, event | category | flops | bytes accessed | tf_op | source)
XLA Modules:
  0.0 138.2 jit_solution(6177262852341944256)
XLA Ops:
  0.0 134.4 %exchange_and_flow.1 = (f32[19,16,16,128]{3,2,1,0:T(8,128)}, f32[2,5,16,128]{3,2,1,0:T(8,128)}, f32[2,5,16,128]{3,2,1,0:T(8,128)}, f32[4,8,128]{2,1,0:T(8,128)}) custom-call(f32[3]{0:T(128)} %force.1, s32[1,128]{1,0:T(1,128)} %bitcast.3, f32[19,128,256]{2,1,0:T(8,128)} %bitcast.2, f32[4,64,128]{2,1,0:T(8,128)} %poro.1, f32[4,64,128]{2,1,0:T(8,128)} %relax.1, ...), custom_call_target="tpu_custom_call" | custom-call | tf_op jit(solution)/shard_map/exchange_and_flow/pallas_call | solution.py:482
  134.4 3.8 %last_stream.1 = f32[19,16,16,128]{3,2,1,0:T(8,128)} custom-call(f32[19,16,16,128]{3,2,1,0:T(8,128)} %get-tuple-element.9.middle, f32[2,5,16,128]{3,2,1,0:T(8,128)} %get-tuple-element.10.x_face, f32[2,5,16,128]{3,2,1,0:T(8,128)} %get-tuple-element.11.y_face, f32[4,8,128]{2,1,0:T(8,128)} %get-tuple-element.12.c_face), custom_call_target="tpu_custom_call" | custom-call | tf_op jit(solution)/shard_map/last_stream/pallas_call | solution.py:525

commit v4 on v3

--- a/solution.py
+++ b/solution.py
@@ -181,7 +181,7 @@
 def flow_kernel(nx, ny, capacity, parts,
                 force, goal, pdf, poro, relax, mask_hbm, middle, x_out, y_out, c_out,
                 table_rows, table, labels, gathered, mask, halves, packed, arrived, places, slots,
-                slot_of, plane, poro_block, relax_block,
+                slot_of, label_of, near_poro, near_relax, near_mask, poro_block, relax_block,
                 first, second, x_send, y_send, c_send, x_recv, y_recv, c_recv,
                 tile_send, tile_recv, label_send, label_recv, cell_send, cell_recv, own, send, recv):
     n = nx * ny
@@ -230,37 +230,22 @@
     down.wait()
     pl.semaphore_wait(barrier, n - 1)
 
-    def tile_copies(o):
-        to, source = partner(o, 1), partner(o, -1)
-        goal = to[0] * ny + to[1]
-        return (
-            pltpu.make_async_remote_copy(
-                src_ref=labels, dst_ref=places.at[me],
-                send_sem=label_send.at[o], recv_sem=label_recv.at[o],
-                device_id=to, device_id_type=MESH,
-            ),
-            pltpu.make_async_remote_copy(
-                src_ref=packed.at[goal], dst_ref=arrived.at[me],
-                send_sem=tile_send.at[o], recv_sem=tile_recv.at[o],
-                device_id=to, device_id_type=MESH,
-            ),
+    def label_copy(o, slot):
+        return pltpu.make_async_remote_copy(
+            src_ref=labels, dst_ref=places.at[slot],
+            send_sem=label_send.at[o], recv_sem=label_recv.at[o],
+            device_id=partner(o, 1), device_id_type=MESH,
         )
 
-    def tile_arrivals(o):
-        to, source = partner(o, 1), partner(o, -1)
-        origin = source[0] * ny + source[1]
-        return (
-            pltpu.make_async_remote_copy(
-                src_ref=labels, dst_ref=places.at[origin],
-                send_sem=label_send.at[o], recv_sem=label_recv.at[o],
-                device_id=to, device_id_type=MESH,
-            ),
-            pltpu.make_async_remote_copy(
-                src_ref=packed.at[origin], dst_ref=arrived.at[origin],
-                send_sem=tile_send.at[o], recv_sem=tile_recv.at[o],
-                device_id=to, device_id_type=MESH,
-            ),
+    def tile_copy(o, source, slot):
+        return pltpu.make_async_remote_copy(
+            src_ref=packed.at[source], dst_ref=arrived.at[slot],
+            send_sem=tile_send.at[o], recv_sem=tile_recv.at[o],
+            device_id=partner(o, 1), device_id_type=MESH,
         )
+
+    def number(device):
+        return device[0] * ny + device[1]
 
     def cell_copies(o, source, target):
         return [
@@ -288,12 +273,16 @@
 
     def send_tiles(step, carry):
         o = order(step)
-        to = partner(o, 1)
-        fill(packed, to[0] * ny + to[1])
-        for copy in tile_copies(o):
-            copy.start()
-        return carry
-
+        goal_device = number(partner(o, 1))
+        fill(packed, goal_device)
+        tile_copy(o, goal_device, me).start()
+        return carry
+
+    def send_labels(step, carry):
+        label_copy(order(step), me).start()
+        return carry
+
+    lax.fori_loop(0, n - 1, send_labels, 0)
     lax.fori_loop(0, n - 1, send_tiles, 0)
     for o in range(1, ny):
         for copy in cell_copies(o, b, lax.rem(b + o, ny)):
@@ -307,13 +296,12 @@
             copy.wait_send()
             copy.wait_recv()
 
-    def take_tiles(step, carry):
-        for copy in tile_arrivals(order(step)):
-            copy.wait_recv()
-        return carry
-
-    lax.fori_loop(0, n - 1, take_tiles, 0)
-
+    def take_labels(step, carry):
+        o = order(step)
+        label_copy(o, number(partner(o, -1))).wait_recv()
+        return carry
+
+    lax.fori_loop(0, n - 1, take_labels, 0)
     chunk, offset = (me * capacity) // LANES, lax.rem(me * capacity, LANES)
 
     def collect(d, carry):
@@ -330,10 +318,40 @@
         found = jnp.maximum(found, jnp.where(label == lane, sender * capacity + k, 0))
     slots[...] = jnp.max(found, axis=0, keepdims=True)
     lift = pltpu.make_async_copy(slots, slot_of, own.at[parts + 4])
+    spread_out = pltpu.make_async_copy(gathered, label_of, own.at[parts + 5])
     lift.start()
+    spread_out.start()
     lift.wait()
+    spread_out.wait()
     forces = [force[axis] for axis in range(3)]
     strips = by // parts
+    cell_rows = [ref.reshape(bx * by, LANES) for ref in (poro_block, relax_block, mask)]
+    size = min(8, depth)
+
+    def collide_block(source):
+        for k in range(capacity):
+            begin = jnp.maximum(label_of[source, offset + k], 0) * parts
+            for rows_of, near in zip(cell_rows, (near_poro, near_relax, near_mask)):
+                near[k * parts : (k + 1) * parts, :] = rows_of[pl.ds(begin, parts), :]
+        for h in range(0, depth, size):
+            dev = [arrived[source, q * depth + h : q * depth + h + size, :] for q in range(19)]
+            near = [ref[h : h + size, :] for ref in (near_poro, near_relax, near_mask)]
+            done = collide(dev, *near, forces)
+            for q in range(19):
+                arrived[source, q * depth + h : q * depth + h + size, :] = done[q]
+
+    collide_block(me)
+
+    def take_tiles(step, carry):
+        o = order(step)
+        source = number(partner(o, -1))
+        tile_copy(o, source, source).wait_recv()
+        collide_block(source)
+        return carry
+
+    lax.fori_loop(0, n - 1, take_tiles, 0)
+    tall = by + 2 * PAD
+    first_rows = first.reshape(19 * (bx + 2) * tall, LANES)
 
     def start(x, carry):
         for j in range(strips):
@@ -341,16 +359,10 @@
             source = lax.div(slot, capacity)
             row = (slot - source * capacity) * parts
             for r in range(parts):
-                plane[pl.ds(j * parts + r, 19, stride=by), :] = arrived[
+                begin = (x + 1) * tall + PAD + j * parts + r
+                first_rows[pl.ds(begin, 19, stride=(bx + 2) * tall), :] = arrived[
                     source, pl.ds(row + r, 19, stride=depth), :
                 ]
-        for h in range(0, by, 8):
-            dev = [plane[q * by + h : q * by + h + 8, :] for q in range(19)]
-            done = collide(
-                dev, poro_block[x, h : h + 8], relax_block[x, h : h + 8], mask[x, h : h + 8], forces
-            )
-            for q in range(19):
-                first[q, x + 1, PAD + h : PAD + h + 8, :] = done[q]
         return carry
 
     lax.fori_loop(0, bx, start, 0)
@@ -409,10 +421,7 @@
             block(x, h)
         return carry
 
-    tall = by + 2 * PAD
-    first_rows = first.reshape(19 * (bx + 2) * tall, LANES)
     second_rows = second.reshape(19 * (bx + 2) * tall, LANES)
-    cell_rows = [ref.reshape(bx * by, LANES) for ref in (poro_block, relax_block, mask)]
 
     def edge(row, x):
         dev = []
@@ -453,8 +462,9 @@
     keep.wait()
 
     def sent(step, carry):
-        for copy in tile_copies(order(step)):
-            copy.wait_send()
+        o = order(step)
+        label_copy(o, me).wait_send()
+        tile_copy(o, number(partner(o, 1)), me).wait_send()
         return carry
 
     lax.fori_loop(0, n - 1, sent, 0)
@@ -497,7 +507,10 @@
             pltpu.VMEM((n, chunks, LANES), jnp.int32),
             pltpu.VMEM((1, LANES), jnp.int32),
             pltpu.SMEM((1, LANES), jnp.int32),
-            pltpu.VMEM((19 * by, nz), jnp.float32),
+            pltpu.SMEM((n, LANES), jnp.int32),
+            pltpu.VMEM((capacity * parts, nz), jnp.float32),
+            pltpu.VMEM((capacity * parts, nz), jnp.float32),
+            pltpu.VMEM((capacity * parts, nz), jnp.int32),
             block,
             block,
             field,
@@ -507,7 +520,7 @@
         + faces
         + [pltpu.SemaphoreType.DMA((n,))] * 4
         + [pltpu.SemaphoreType.DMA((2 * ny,))] * 2
-        + [pltpu.SemaphoreType.DMA((parts + 5,))]
+        + [pltpu.SemaphoreType.DMA((parts + 6,))]
         + [pltpu.SemaphoreType.DMA((2, 8))] * 2,
         compiler_params=pltpu.CompilerParams(
             collective_id=0, has_side_effects=True, vmem_limit_bytes=62 * MIB

time: 138 us -> 139 us (level)
  no operation moved by 1% of the time
where the time goes in v4:
time: 139 us
  Pallas kernels  139 us (100%)
    pallas_call x1, Pallas kernels, local(): pl.pallas_call(functools.partial(flow_kernel, nx, ny, capacity, parts), o...  135 us
    pallas_call x1, Pallas kernels, local(): pl.pallas_call(functools.partial(finish_kernel, pieces), out_shape=result...  3.79 us

profile of v4, /device:TPU:0, one launch (start us, length us, event | category | flops | bytes accessed | tf_op | source)
XLA Modules:
  0.0 139.0 jit_solution(1032468518251826195)
XLA Ops:
  0.0 135.2 %exchange_and_flow.1 = (f32[19,16,16,128]{3,2,1,0:T(8,128)}, f32[2,5,16,128]{3,2,1,0:T(8,128)}, f32[2,5,16,128]{3,2,1,0:T(8,128)}, f32[4,8,128]{2,1,0:T(8,128)}) custom-call(f32[3]{0:T(128)} %force.1, s32[1,128]{1,0:T(1,128)} %bitcast.3, f32[19,128,256]{2,1,0:T(8,128)} %bitcast.2, f32[4,64,128]{2,1,0:T(8,128)} %poro.1, f32[4,64,128]{2,1,0:T(8,128)} %relax.1, ...), custom_call_target="tpu_custom_call" | custom-call | tf_op jit(solution)/shard_map/exchange_and_flow/pallas_call | solution.py:492
  135.2 3.8 %last_stream.1 = f32[19,16,16,128]{3,2,1,0:T(8,128)} custom-call(f32[19,16,16,128]{3,2,1,0:T(8,128)} %get-tuple-element.9.middle, f32[2,5,16,128]{3,2,1,0:T(8,128)} %get-tuple-element.10.x_face, f32[2,5,16,128]{3,2,1,0:T(8,128)} %get-tuple-element.11.y_face, f32[4,8,128]{2,1,0:T(8,128)} %get-tuple-element.12.c_face), custom_call_target="tpu_custom_call" | custom-call | tf_op jit(solution)/shard_map/last_stream/pallas_call | solution.py:538

commit v5 on v4

--- a/solution.py
+++ b/solution.py
@@ -181,7 +181,7 @@
 def flow_kernel(nx, ny, capacity, parts,
                 force, goal, pdf, poro, relax, mask_hbm, middle, x_out, y_out, c_out,
                 table_rows, table, labels, gathered, mask, halves, packed, arrived, places, slots,
-                slot_of, label_of, near_poro, near_relax, near_mask, poro_block, relax_block,
+                slot_of, label_of, plane, near_poro, near_relax, near_mask, poro_block, relax_block,
                 first, second, x_send, y_send, c_send, x_recv, y_recv, c_recv,
                 tile_send, tile_recv, label_send, label_recv, cell_send, cell_recv, own, send, recv):
     n = nx * ny
@@ -359,10 +359,11 @@
             source = lax.div(slot, capacity)
             row = (slot - source * capacity) * parts
             for r in range(parts):
-                begin = (x + 1) * tall + PAD + j * parts + r
-                first_rows[pl.ds(begin, 19, stride=(bx + 2) * tall), :] = arrived[
+                plane[pl.ds(j * parts + r, 19, stride=by), :] = arrived[
                     source, pl.ds(row + r, 19, stride=depth), :
                 ]
+        for q in range(19):
+            first[q, x + 1, PAD : PAD + by, :] = plane[q * by : (q + 1) * by, :]
         return carry
 
     lax.fori_loop(0, bx, start, 0)
@@ -508,6 +509,7 @@
             pltpu.VMEM((1, LANES), jnp.int32),
             pltpu.SMEM((1, LANES), jnp.int32),
             pltpu.SMEM((n, LANES), jnp.int32),
+            pltpu.VMEM((19 * by, nz), jnp.float32),
             pltpu.VMEM((capacity * parts, nz), jnp.float32),
             pltpu.VMEM((capacity * parts, nz), jnp.float32),
             pltpu.VMEM((capacity * parts, nz), jnp.int32),

time: 139 us -> 138 us (level)
  no operation moved by 1% of the time
where the time goes in v5:
time: 138 us
  Pallas kernels  138 us (100%)
    pallas_call x1, Pallas kernels, local(): pl.pallas_call(functools.partial(flow_kernel, nx, ny, capacity, parts), o...  134 us
    pallas_call x1, Pallas kernels, local(): pl.pallas_call(functools.partial(finish_kernel, pieces), out_shape=result...  3.79 us

profile of v5, /device:TPU:0, one launch (start us, length us, event | category | flops | bytes accessed | tf_op | source)
XLA Modules:
  0.0 138.1 jit_solution(14819077520272335970)
XLA Ops:
  0.0 134.3 %exchange_and_flow.1 = (f32[19,16,16,128]{3,2,1,0:T(8,128)}, f32[2,5,16,128]{3,2,1,0:T(8,128)}, f32[2,5,16,128]{3,2,1,0:T(8,128)}, f32[4,8,128]{2,1,0:T(8,128)}) custom-call(f32[3]{0:T(128)} %force.1, s32[1,128]{1,0:T(1,128)} %bitcast.3, f32[19,128,256]{2,1,0:T(8,128)} %bitcast.2, f32[4,64,128]{2,1,0:T(8,128)} %poro.1, f32[4,64,128]{2,1,0:T(8,128)} %relax.1, ...), custom_call_target="tpu_custom_call" | custom-call | tf_op jit(solution)/shard_map/exchange_and_flow/pallas_call | solution.py:493
  134.3 3.8 %last_stream.1 = f32[19,16,16,128]{3,2,1,0:T(8,128)} custom-call(f32[19,16,16,128]{3,2,1,0:T(8,128)} %get-tuple-element.9.middle, f32[2,5,16,128]{3,2,1,0:T(8,128)} %get-tuple-element.10.x_face, f32[2,5,16,128]{3,2,1,0:T(8,128)} %get-tuple-element.11.y_face, f32[4,8,128]{2,1,0:T(8,128)} %get-tuple-element.12.c_face), custom_call_target="tpu_custom_call" | custom-call | tf_op jit(solution)/shard_map/last_stream/pallas_call | solution.py:540
